TPU v7x, 32 devices: a whole 2x2x4 slice. The times are simulated.
32 devices in a mesh: prow: 4 (over y, x), pcol: 8 (over z, core).
Axes of the slice: x: 2, y: 2, z: 4, core: 2. Of those that a mesh axis runs over, the one named last changes fastest.
Arguments:
- latent: bfloat16 [16, 32, 1280], P('prow', 'pcol'), may hold values from -8 to 8
- norm_scale: float32 [3, 1280], replicated, may hold values from 0.25 to 1.75
- norm_shift: float32 [3, 1280], replicated, may hold values from -3 to 3
- time_shift: float32 [1280], replicated, may hold values from -4 to 4
- conv_bias: float32 [2, 1280], replicated, may hold values from -3 to 3
- conv_one: bfloat16 [3, 3, 1280, 1280], P(None, None, 'prow'), may hold values from -0.0546875 to 0.0546875
- conv_two: bfloat16 [3, 3, 1280, 1280], P(None, None, 'prow'), may hold values from -0.0546875 to 0.0546875
- w_qkv: bfloat16 [768, 1280], P('prow'), may hold values from -0.3125 to 0.3125
- w_out: bfloat16 [1280, 256], P('prow'), may hold values from -0.375 to 0.375
- stale_kv: bfloat16 [16, 32, 4, 128], P(None, 'pcol', 'prow'), may hold values from -36 to 36
Outputs:
- next_latent: bfloat16 [16, 32, 1280], P('prow', 'pcol')
- fresh_kv: bfloat16 [16, 32, 4, 128], P(None, 'pcol', 'prow')
All inputs are finite; a program needn't handle non-finite values.
Results may differ from a plain program's by a relative error of at most 0.028.
Values may be sent and summed in bfloat16 or wider, within the bound.
A program may use at most 64 MiB of HBM per device.

v0:
```python
import jax
import jax.numpy as jnp
from jax import lax
from jax.sharding import PartitionSpec as P

GROUPS = 32
HEAD = 64


EPSILON = 1e-05


def padded(cells, sides, width):
    for axis, dim in sides:
        count = lax.axis_size(axis)
        ends = count - 1
        head = lax.slice_in_dim(cells, 0, width, axis=dim)
        tail = lax.slice_in_dim(cells, cells.shape[dim] - width, cells.shape[dim], axis=dim)
        cells = jnp.concatenate(
            [
                lax.ppermute(tail, axis, [(i, (i + 1) % count) for i in range(ends)]),
                cells,
                lax.ppermute(head, axis, [((i + 1) % count, i) for i in range(ends)]),
            ],
            axis=dim,
        )
    return cells


def times_rows(left, right):
    return lax.dot_general(
        left, right, (((1,), (1,)), ((), ())), preferred_element_type=jnp.float32
    )


def group_norm(field, scale, shift, population):
    rows_here, cols_here, width = field.shape
    grouped = field.reshape(rows_here * cols_here, GROUPS, width // GROUPS)
    summed, squared = lax.psum(
        (jnp.sum(grouped, axis=(0, 2)), jnp.sum(grouped * grouped, axis=(0, 2))), ("prow", "pcol")
    )
    average = summed / population
    variance = squared / population - average * average
    centered = grouped - average[None, :, None]
    normed = centered * lax.rsqrt(variance + EPSILON)[None, :, None]
    return normed.reshape(field.shape) * scale + shift


def conv_terms(field, weight):
    rows_here, cols_here, width = field.shape
    out_width = weight.shape[2]
    parties = lax.axis_size("prow")
    cells = rows_here * cols_here
    framed_patch = padded(field, (("prow", 0), ("pcol", 1)), 1)
    stacked = lax.all_gather(framed_patch[None], "prow", axis=0, tiled=True)
    total = jnp.zeros((parties * cells, out_width), jnp.float32)
    for row_tap in range(3):
        for col_tap in range(3):
            total = total + times_rows(
                stacked[:, row_tap : row_tap + rows_here, col_tap : col_tap + cols_here, :].reshape(
                    -1, width
                ),
                weight[row_tap, col_tap],
            )
    returned = lax.all_to_all(
        total.reshape(parties, cells, out_width).astype(jnp.bfloat16),
        "prow",
        split_axis=0,
        concat_axis=2,
        tiled=True,
    ).astype(jnp.float32)
    return returned.reshape(cells, parties * out_width)


def partial_softmax(queries, pairs, scale):
    keys = pairs[..., :HEAD]
    values = pairs[..., HEAD:]
    scores = jnp.einsum("qhd,khd->hqk", queries, keys, preferred_element_type=jnp.float32) * scale
    highest = jnp.max(scores, axis=-1)
    weights = jnp.exp(scores - highest[..., None])
    denominator = jnp.sum(weights, axis=-1)
    weighted = jnp.einsum(
        "hqk,khd->qhd", weights.astype(jnp.bfloat16), values, preferred_element_type=jnp.float32
    )
    return (highest, denominator, weighted)


def shards(
    latent,
    norm_scale,
    norm_shift,
    time_shift,
    conv_bias,
    conv_one,
    conv_two,
    w_qkv,
    w_out,
    stale_kv,
):
    rows_here, cols_here, width = latent.shape
    cells = rows_here * cols_here
    parties = lax.axis_size("prow")
    population = float(cells * lax.axis_size("prow") * lax.axis_size("pcol") * (width // GROUPS))
    inputs = latent.astype(jnp.float32)
    first_act = jax.nn.silu(group_norm(inputs, norm_scale[0], norm_shift[0], population)).astype(
        jnp.bfloat16
    )
    first_conv = conv_terms(first_act, conv_one).reshape(latent.shape) + conv_bias[0] + time_shift
    second_act = jax.nn.silu(
        group_norm(first_conv, norm_scale[1], norm_shift[1], population)
    ).astype(jnp.bfloat16)
    second_conv = conv_terms(second_act, conv_two).reshape(latent.shape) + conv_bias[1]
    resnet_out = (inputs + second_conv).astype(jnp.bfloat16)
    attn_in = group_norm(
        resnet_out.astype(jnp.float32), norm_scale[2], norm_shift[2], population
    ).astype(jnp.bfloat16)
    column_width = w_qkv.shape[0]
    heads_here = column_width // (3 * HEAD)
    piece = lax.all_gather(attn_in, "prow", axis=0, tiled=True)
    mapped = times_rows(piece.reshape(-1, width), w_qkv)
    strip_qkv = mapped.astype(jnp.bfloat16).reshape(piece.shape[0], cols_here, column_width)
    strip_rows = strip_qkv.shape[0]
    parted = strip_qkv.reshape(strip_rows * cols_here, heads_here, 3, HEAD)
    queries = parted[:, :, 0, :]
    fresh = jnp.concatenate([parted[:, :, 1, :], parted[:, :, 2, :]], axis=-1)
    scale = HEAD ** (-0.5)
    column = lax.axis_index("pcol")
    initial = partial_softmax(queries, fresh, scale)
    piece = lax.all_gather(stale_kv, "pcol", axis=1, tiled=True)
    highest, denominator, weighted = initial
    columns = lax.iota(jnp.int32, piece.shape[1])
    foreign = jnp.broadcast_to((columns // cols_here != column)[None, :], piece.shape[:2]).reshape(
        -1
    )
    pairs = piece.reshape(-1, heads_here, 2 * HEAD)
    scores = (
        jnp.einsum("qhd,khd->hqk", queries, pairs[:, :, :HEAD], preferred_element_type=jnp.float32)
        * scale
    )
    scores = jnp.where(foreign[None, None, :], scores, -jnp.inf)
    raised = jnp.maximum(highest, jnp.max(scores, axis=-1))
    factor = jnp.exp(highest - raised)
    weights = jnp.exp(scores - raised[..., None])
    denominator = denominator * factor + jnp.sum(weights, axis=-1)
    update = jnp.einsum(
        "hqk,khd->qhd",
        weights.astype(jnp.bfloat16),
        pairs[:, :, HEAD:],
        preferred_element_type=jnp.float32,
    )
    weighted = weighted * factor.T[..., None] + update
    highest, denominator, weighted = (raised, denominator, weighted)
    attended = (
        (weighted / denominator.T[..., None]).astype(jnp.bfloat16).reshape(-1, heads_here * HEAD)
    )
    out_width = w_out.shape[0]
    summed = times_rows(lax.all_gather(attended, "prow", axis=1, tiled=True), w_out)
    added = (
        lax.all_to_all(
            summed.reshape(parties, cells, out_width).astype(jnp.bfloat16),
            "prow",
            split_axis=0,
            concat_axis=2,
            tiled=True,
        )
        .astype(jnp.float32)
        .reshape(cells, width)
    )
    next_latent = (
        (resnet_out.astype(jnp.float32).reshape(cells, width) + added)
        .astype(jnp.bfloat16)
        .reshape(latent.shape)
    )
    return (next_latent, fresh.reshape(strip_rows, cols_here, heads_here, 2 * HEAD))


def solution(mesh):
    placed = (
        P("prow", "pcol", None),
        P(),
        P(),
        P(),
        P(),
        P(None, None, "prow", None),
        P(None, None, "prow", None),
        P("prow", None),
        P("prow", None),
        P(None, "pcol", "prow", None),
    )
    return jax.shard_map(
        shards,
        mesh=mesh,
        in_specs=placed,
        out_specs=(P("prow", "pcol", None), P(None, "pcol", "prow", None)),
        check_vma=False,
    )
```

profile of v0, /device:TPU:0, one launch (start us, length us, event | category | flops | bytes accessed | tf_op | source)
XLA Modules:
  0.0 267.6 jit_solution(10719249236742011187)
XLA Ops:
  0.6 0.9 convert_reduce_fusion.1
  1.9 42.0 %all-reduce.2 = (f32[32]{0:T(128)S(1)}, f32[32]{0:T(128)S(1)}) all-reduce(f32[32]{0:T(128)S(1)} %reduce_sum.96, f32[32]{0:T(128)S(1)} %reduce_sum.90), channel_id=1, replica_groups=mesh['prow'=4,'pcol'=8] {'prow','pcol'}, use_global_device_ids=true, to_apply=%region_5.6 | all-reduce | flops 64 | bytes 512 | tf_op jit(solution)/shard_map/psum | solution.py:39
  44.3 0.9 slice_reduce_fusion
  45.2 0.9 fusion.64
  46.1 4.2 %collective-permute-start = (bf16[1,4,1280]{2,1,0:T(4,128)(2,1)S(1)}, bf16[1,4,1280]{2,1,0:T(4,128)(2,1)S(1)}, u32[]{:S(2)}, u32[]{:S(2)}) collective-permute-start(bf16[1,4,1280]{2,1,0:T(4,128)(2,1)S(1)} %get-tuple-element.59), channel_id=1, source_target_pairs={{0,8},{8,16},{16,24},{1,9},{9,17},{17,25},{2,10},{10,18},{18,26},{... | collective-permute-start | bytes 30728 | tf_op jit(solution)/shard_map/ppermute | solution.py:21
  50.3 1.3 collective-permute-start.1
  51.7 4.2 %collective-permute-done.1 = bf16[1,4,1280]{2,1,0:T(4,128)(2,1)S(1)} collective-permute-done((bf16[1,4,1280]{2,1,0:T(4,128)(2,1)S(1)}, bf16[1,4,1280]{2,1,0:T(4,128)(2,1)S(1)}, u32[]{:S(2)}, u32[]{:S(2)}) %collective-permute-start.1) | collective-permute-done | bytes 10272 | tf_op jit(solution)/shard_map/ppermute | solution.py:23
  56.0 1.3 collective-permute-start.2
  57.3 1.3 collective-permute-start.3
  58.6 3.5 %collective-permute-done.3 = bf16[6,1,1280]{2,1,0:T(2,128)(2,1)S(1)} collective-permute-done((bf16[6,1,1280]{2,1,0:T(2,128)(2,1)S(1)}, bf16[6,1,1280]{2,1,0:T(2,128)(2,1)S(1)}, u32[]{:S(2)}, u32[]{:S(2)}) %collective-permute-start.3) | collective-permute-done | bytes 15392 | tf_op jit(solution)/shard_map/ppermute | solution.py:23
  62.2 10.8 %all-gather = bf16[24,6,1280]{2,1,0:T(8,128)(2,1)S(1)} all-gather(bf16[6,6,1280]{2,1,0:T(8,128)(2,1)S(1)} %pad_maximum_fusion), channel_id=2, replica_groups=mesh['prow'=4,'pcol'=8] {'prow'}, dimensions={0}, use_global_device_ids=true | all-gather | bytes 460800 | tf_op jit(solution)/shard_map/all_gather | solution.py:55
  73.9 1.5 fusion.26
  75.5 1.5 convolution_add_fusion.15
  77.0 1.5 convolution_add_fusion.14
  78.5 1.5 convolution_add_fusion.13
  80.0 1.5 convolution_add_fusion.12
  81.5 1.5 convolution_add_fusion.11
  83.0 1.5 convolution_add_fusion.10
  84.5 1.5 convolution_add_fusion.9
  86.1 2.1 fusion.1
  88.2 3.3 %all-to-all-start = ((bf16[4,16,320]{2,1,0:T(8,128)(2,1)}), bf16[4,16,320]{2,1,0:T(8,128)(2,1)S(1)}, u32[]{:S(2)}, u32[]{:S(2)}) async-start(bf16[4,16,320]{2,1,0:T(8,128)(2,1)} %bitcast.10), calls=%async_computation | async-start | bytes 98304 | tf_op jit(solution)/shard_map/all_to_all | solution.py:65
  91.7 4.6 %all-to-all-done = bf16[4,16,320]{2,1,0:T(8,128)(2,1)S(1)} async-done(((bf16[4,16,320]{2,1,0:T(8,128)(2,1)}), bf16[4,16,320]{2,1,0:T(8,128)(2,1)S(1)}, u32[]{:S(2)}, u32[]{:S(2)}) %all-to-all-start) | async-done | bytes 40992 | tf_op jit(solution)/shard_map/all_to_all | solution.py:65
  96.7 41.3 %all-reduce.1 = (f32[32]{0:T(128)S(1)}, f32[32]{0:T(128)S(1)}) all-reduce(f32[32]{0:T(128)S(1)} %reduce_sum.125, f32[32]{0:T(128)S(1)} %reduce_sum.99), channel_id=1, replica_groups=mesh['prow'=4,'pcol'=8] {'prow','pcol'}, use_global_device_ids=true, to_apply=%region_11.12 | all-reduce | flops 64 | bytes 512 | tf_op jit(solution)/shard_map/psum | solution.py:39
  138.6 4.2 %collective-permute-start.4 = (bf16[1,4,1280]{2,1,0:T(4,128)(2,1)S(1)}, bf16[1,4,1280]{2,1,0:T(4,128)(2,1)S(1)}, u32[]{:S(2)}, u32[]{:S(2)}) collective-permute-start(bf16[1,4,1280]{2,1,0:T(4,128)(2,1)S(1)} %get-tuple-element.57), channel_id=1, source_target_pairs={{0,8},{8,16},{16,24},{1,9},{9,17},{17,25},{2,10},{10,18},{18,26},{... | collective-permute-start | bytes 30728 | tf_op jit(solution)/shard_map/ppermute | solution.py:21
  142.8 1.3 collective-permute-start.5
  144.2 4.2 %collective-permute-done.5 = bf16[1,4,1280]{2,1,0:T(4,128)(2,1)S(1)} collective-permute-done((bf16[1,4,1280]{2,1,0:T(4,128)(2,1)S(1)}, bf16[1,4,1280]{2,1,0:T(4,128)(2,1)S(1)}, u32[]{:S(2)}, u32[]{:S(2)}) %collective-permute-start.5) | collective-permute-done | bytes 10272 | tf_op jit(solution)/shard_map/ppermute | solution.py:23
  148.5 1.3 collective-permute-start.6
  149.8 1.3 collective-permute-start.7
  151.1 1.9 collective-permute-done.7
  153.2 10.8 %all-gather.1 = bf16[24,6,1280]{2,1,0:T(8,128)(2,1)S(1)} all-gather(bf16[6,6,1280]{2,1,0:T(8,128)(2,1)S(1)} %pad_maximum_fusion.1), channel_id=3, replica_groups=mesh['prow'=4,'pcol'=8] {'prow'}, dimensions={0}, use_global_device_ids=true | all-gather | bytes 460800 | tf_op jit(solution)/shard_map/all_gather | solution.py:55
  164.9 1.5 fusion.16
  166.4 1.5 convolution_add_fusion.7
  167.9 1.5 convolution_add_fusion.6
  169.5 1.5 convolution_add_fusion.5
  171.0 1.5 convolution_add_fusion.4
  172.5 1.5 convolution_add_fusion.3
  174.0 1.5 convolution_add_fusion.2
  175.5 1.5 convolution_add_fusion.1
  177.0 2.1 fusion.2
  179.2 3.3 %all-to-all-start.1 = ((bf16[4,16,320]{2,1,0:T(8,128)(2,1)}), bf16[4,16,320]{2,1,0:T(8,128)(2,1)S(1)}, u32[]{:S(2)}, u32[]{:S(2)}) async-start(bf16[4,16,320]{2,1,0:T(8,128)(2,1)} %bitcast.25), calls=%async_computation.1 | async-start | bytes 98304 | tf_op jit(solution)/shard_map/all_to_all | solution.py:65
  182.5 15.5 %all_gather.18 = bf16[16,32,1,128]{3,0,2,1:T(8,128)(2,1)S(1)} all-gather(bf16[16,4,1,128]{3,0,2,1:T(8,128)(2,1)S(1)} %copy.60), channel_id=1, replica_groups=mesh['prow'=4,'pcol'=8] {'pcol'}, dimensions={1}, use_global_device_ids=true | all-gather | bytes 147456 | tf_op jit(solution)/shard_map/all_gather | solution.py:129
  198.8 40.1 %all-reduce = (f32[32]{0:T(128)S(1)}, f32[32]{0:T(128)S(1)}) all-reduce(f32[32]{0:T(128)S(1)} %reduce_sum.131, f32[32]{0:T(128)S(1)} %reduce_sum.128), channel_id=1, replica_groups=mesh['prow'=4,'pcol'=8] {'prow','pcol'}, use_global_device_ids=true, to_apply=%region_17.18 | all-reduce | flops 64 | bytes 512 | tf_op jit(solution)/shard_map/psum | solution.py:39
  239.2 9.4 %all_gather.17 = bf16[16,4,1280]{2,1,0:T(4,128)(2,1)S(1)} all-gather(bf16[4,4,1280]{2,1,0:T(4,128)(2,1)S(1)} %fusion.61), channel_id=1, replica_groups=mesh['prow'=4,'pcol'=8] {'prow'}, dimensions={0}, use_global_device_ids=true | all-gather | bytes 204800 | tf_op jit(solution)/shard_map/all_gather | solution.py:119
  250.5 7.4 %all-gather.2 = bf16[64,1,256]{0,2,1:T(8,128)(2,1)S(1)} all-gather(bf16[64,1,64]{0,2,1:T(8,128)(2,1)S(1)} %fusion.7), channel_id=4, replica_groups=mesh['prow'=4,'pcol'=8] {'prow'}, dimensions={2}, use_global_device_ids=true | all-gather | bytes 40960 | tf_op jit(solution)/shard_map/all_gather | solution.py:157
  257.9 0.8 convolution_convert_fusion
  258.7 3.3 %all-to-all-start.2 = ((bf16[4,16,320]{2,1,0:T(8,128)(2,1)}), bf16[4,16,320]{2,1,0:T(8,128)(2,1)S(1)}, u32[]{:S(2)}, u32[]{:S(2)}) async-start(bf16[4,16,320]{2,1,0:T(8,128)(2,1)} %bitcast.40), calls=%async_computation.2 | async-start | bytes 98304 | tf_op jit(solution)/shard_map/all_to_all | solution.py:159
  262.0 0.7 maximum_bitcast_fusion
  262.7 4.1 %all-to-all-done.2 = bf16[4,16,320]{2,1,0:T(8,128)(2,1)S(1)} async-done(((bf16[4,16,320]{2,1,0:T(8,128)(2,1)}), bf16[4,16,320]{2,1,0:T(8,128)(2,1)S(1)}, u32[]{:S(2)}, u32[]{:S(2)}) %all-to-all-start.2) | async-done | bytes 40992 | tf_op jit(solution)/shard_map/all_to_all | solution.py:159
  (108 shorter events, 8.0 us)
Async XLA Ops:
  0.6 248.0 %copy-start = (bf16[192,1280]{1,0:T(8,128)(2,1)S(1)}, bf16[192,1280]{1,0:T(8,128)(2,1)}, u32[]{:S(2)}) copy-start(bf16[192,1280]{1,0:T(8,128)(2,1)} %param.17) | copy-start | bytes 1474564
  46.1 5.6 %collective-permute-start = (bf16[1,4,1280]{2,1,0:T(4,128)(2,1)S(1)}, bf16[1,4,1280]{2,1,0:T(4,128)(2,1)S(1)}, u32[]{:S(2)}, u32[]{:S(2)}) collective-permute-start(bf16[1,4,1280]{2,1,0:T(4,128)(2,1)S(1)} %get-tuple-element.59), channel_id=1, source_target_pairs={{0,8},{8,16},{16,24},{1,9},{9,17},{17,25},{2,10},{10,18},{18,26},{... | collective-permute-start | bytes 30728 | tf_op jit(solution)/shard_map/ppermute | solution.py:21
  50.3 5.6 %collective-permute-start.1 = (bf16[1,4,1280]{2,1,0:T(4,128)(2,1)S(1)}, bf16[1,4,1280]{2,1,0:T(4,128)(2,1)S(1)}, u32[]{:S(2)}, u32[]{:S(2)}) collective-permute-start(bf16[1,4,1280]{2,1,0:T(4,128)(2,1)S(1)} %get-tuple-element.60), channel_id=1, source_target_pairs={{8,0},{16,8},{24,16},{9,1},{17,9},{25,17},{10,2},{18,10},{26,18},{... | collective-permute-start | bytes 30728 | tf_op jit(solution)/shard_map/ppermute | solution.py:23
  56.0 2.6 collective-permute-start.2
  57.3 4.8 %collective-permute-start.3 = (bf16[6,1,1280]{2,1,0:T(2,128)(2,1)S(1)}, bf16[6,1,1280]{2,1,0:T(2,128)(2,1)S(1)}, u32[]{:S(2)}, u32[]{:S(2)}) collective-permute-start(bf16[6,1,1280]{2,1,0:T(2,128)(2,1)S(1)} %get-tuple-element.54), channel_id=1, source_target_pairs={{1,0},{2,1},{3,2},{4,3},{5,4},{6,5},{7,6},{9,8},{10,9},{11,10},{12... | collective-permute-start | bytes 46088 | tf_op jit(solution)/shard_map/ppermute | solution.py:23
  73.5 18.0 %copy-start.5 = (f32[2,1280]{1,0:T(2,128)S(1)}, f32[2,1280]{1,0:T(2,128)}, u32[]{:S(2)}) copy-start(f32[2,1280]{1,0:T(2,128)} %param.14) | copy-start | bytes 30724
  73.5 18.1 %copy-start.3 = (f32[1280]{0:T(1024)S(1)}, f32[1280]{0:T(1024)}, u32[]{:S(2)}) copy-start(f32[1280]{0:T(1024)} %param.13) | copy-start | bytes 15364
  73.5 77.6 %copy-start.4 = (bf16[16,4,1,128]{3,1,2,0:T(4,128)(2,1)S(1)}, bf16[16,4,1,128]{3,1,2,0:T(4,128)(2,1)}, u32[]{:S(2)}) copy-start(bf16[16,4,1,128]{3,1,2,0:T(4,128)(2,1)} %param.19) | copy-start | bytes 49156
  88.2 8.0 %all-to-all-start = ((bf16[4,16,320]{2,1,0:T(8,128)(2,1)}), bf16[4,16,320]{2,1,0:T(8,128)(2,1)S(1)}, u32[]{:S(2)}, u32[]{:S(2)}) async-start(bf16[4,16,320]{2,1,0:T(8,128)(2,1)} %bitcast.10), calls=%async_computation | async-start | bytes 98304 | tf_op jit(solution)/shard_map/all_to_all | solution.py:65
  138.6 5.6 %collective-permute-start.4 = (bf16[1,4,1280]{2,1,0:T(4,128)(2,1)S(1)}, bf16[1,4,1280]{2,1,0:T(4,128)(2,1)S(1)}, u32[]{:S(2)}, u32[]{:S(2)}) collective-permute-start(bf16[1,4,1280]{2,1,0:T(4,128)(2,1)S(1)} %get-tuple-element.57), channel_id=1, source_target_pairs={{0,8},{8,16},{16,24},{1,9},{9,17},{17,25},{2,10},{10,18},{18,26},{... | collective-permute-start | bytes 30728 | tf_op jit(solution)/shard_map/ppermute | solution.py:21
  142.8 5.6 %collective-permute-start.5 = (bf16[1,4,1280]{2,1,0:T(4,128)(2,1)S(1)}, bf16[1,4,1280]{2,1,0:T(4,128)(2,1)S(1)}, u32[]{:S(2)}, u32[]{:S(2)}) collective-permute-start(bf16[1,4,1280]{2,1,0:T(4,128)(2,1)S(1)} %get-tuple-element.58), channel_id=1, source_target_pairs={{8,0},{16,8},{24,16},{9,1},{17,9},{25,17},{10,2},{18,10},{26,18},{... | collective-permute-start | bytes 30728 | tf_op jit(solution)/shard_map/ppermute | solution.py:23
  148.5 2.6 collective-permute-start.6
  149.8 3.3 %collective-permute-start.7 = (bf16[6,1,1280]{2,1,0:T(2,128)(2,1)S(1)}, bf16[6,1,1280]{2,1,0:T(2,128)(2,1)S(1)}, u32[]{:S(2)}, u32[]{:S(2)}) collective-permute-start(bf16[6,1,1280]{2,1,0:T(2,128)(2,1)S(1)} %get-tuple-element.52), channel_id=1, source_target_pairs={{1,0},{2,1},{3,2},{4,3},{5,4},{6,5},{7,6},{9,8},{10,9},{11,10},{12... | collective-permute-start | bytes 46088 | tf_op jit(solution)/shard_map/ppermute | solution.py:23
  164.4 33.8 %copy-start.1 = (bf16[4,4,1280]{2,1,0:T(4,128)(2,1)S(1)}, bf16[4,4,1280]{2,1,0:T(4,128)(2,1)}, u32[]{:S(2)}) copy-start(bf16[4,4,1280]{2,1,0:T(4,128)(2,1)} %param.10) | copy-start | bytes 122884
  164.8 93.0 %copy-start.2 = (bf16[320,256]{1,0:T(8,128)(2,1)S(1)}, bf16[320,256]{1,0:T(8,128)(2,1)}, u32[]{:S(2)}) copy-start(bf16[320,256]{1,0:T(8,128)(2,1)} %param.18) | copy-start | bytes 491524
  179.2 18.8 %all-to-all-start.1 = ((bf16[4,16,320]{2,1,0:T(8,128)(2,1)}), bf16[4,16,320]{2,1,0:T(8,128)(2,1)S(1)}, u32[]{:S(2)}, u32[]{:S(2)}) async-start(bf16[4,16,320]{2,1,0:T(8,128)(2,1)} %bitcast.25), calls=%async_computation.1 | async-start | bytes 98304 | tf_op jit(solution)/shard_map/all_to_all | solution.py:65
  258.7 8.0 %all-to-all-start.2 = ((bf16[4,16,320]{2,1,0:T(8,128)(2,1)}), bf16[4,16,320]{2,1,0:T(8,128)(2,1)S(1)}, u32[]{:S(2)}, u32[]{:S(2)}) async-start(bf16[4,16,320]{2,1,0:T(8,128)(2,1)} %bitcast.40), calls=%async_computation.2 | async-start | bytes 98304 | tf_op jit(solution)/shard_map/all_to_all | solution.py:159
where the time goes:
time: 269 us; the launch traced here: 268 us
  blocking collectives  177 us (66%)
  matrix products  30.5 us (11%)
  starting transfers between devices  25.9 us (10%)
  waiting for transfers between devices  22.6 us (8%)
  local copies, waits for them, and re-layouts  5.44 us (2%)
  other arithmetic  4.62 us (2%)
    psum x3, blocking collectives, group_norm(): lax.psum((jnp.sum(grouped, axis=(0, 2)), jnp.sum(grouped * grouped, axis=...  123 us
    dot_general x20, matrix products, times_rows(): lax.dot_general(left, right, (((1,), (1,)), ((), ())), preferred_element_...  29.5 us
    all_gather x2, blocking collectives, conv_terms(): stacked = lax.all_gather(framed_patch[None], 'prow', axis=0, tiled=True)  21.6 us
    all_gather x1, blocking collectives, shards(): piece = lax.all_gather(stale_kv, 'pcol', axis=1, tiled=True)  15.5 us
    ppermute x4, waiting for transfers between devices, padded(): lax.ppermute(head, axis, [((i + 1) % count, i) for i in range(ends)])  13.8 us
    ppermute x4, starting transfers between devices, padded(): lax.ppermute(tail, axis, [(i, (i + 1) % count) for i in range(ends)])  10.9 us
    all_gather x1, blocking collectives, shards(): piece = lax.all_gather(attn_in, 'prow', axis=0, tiled=True)  9.36 us
    all_gather x1, blocking collectives, shards(): lax.all_gather(attended, 'prow', axis=1, tiled=True)  7.36 us
  transfers between devices with their start and end apart: 11, of which 8 were waited for; matrix products, arithmetic and copies ran while one was open for 0% of the time, Pallas kernels for 0%

commit v1 on v0

--- a/solution.py
+++ b/solution.py
@@ -1,6 +1,10 @@
+import functools
+
 import jax
 import jax.numpy as jnp
 from jax import lax
+from jax.experimental import pallas as pl
+from jax.experimental.pallas import tpu as pltpu
 from jax.sharding import PartitionSpec as P
 
 GROUPS = 32
@@ -174,6 +178,508 @@
     return (next_latent, fresh.reshape(strip_rows, cols_here, heads_here, 2 * HEAD))
 
 
+LANES = 256
+MESH = pl.DeviceIdType.MESH
+BF = jnp.bfloat16
+F32 = jnp.float32
+
+
+def fits(mesh, latent, *rest):
+    rows, cols, width = latent.shape
+    conv_one, w_qkv, w_out = rest[4], rest[6], rest[7]
+    rows_all = rows * mesh.shape["prow"]
+    block = conv_one.shape[2]
+    return (
+        mesh.size <= 64
+        and rows_all % 16 == 0
+        and (rows * cols) % 16 == 0
+        and width % LANES == 0
+        and block % (width // GROUPS) == 0
+        and w_qkv.shape[0] == 3 * HEAD
+        and w_out.shape[0] == block
+        and 4 * conv_one.size < 32 * 2**20
+    )
+
+
+def matmul(left, right):
+    return lax.dot_general(left, right, (((1,), (0,)), ((), ())), preferred_element_type=F32)
+
+
+def iota2(shape, dim):
+    return lax.broadcasted_iota(jnp.int32, shape, dim)
+
+
+def one_hot(mask):
+    return jnp.where(mask, 1.0, 0.0).astype(BF)
+
+
+def split_terms(value):
+    high = value.astype(BF)
+    rest = value - high.astype(F32)
+    middle = rest.astype(BF)
+    low = (rest - middle.astype(F32)).astype(BF)
+    return high, middle, low
+
+
+def remote(src, dst, send, recv, row, col):
+    return pltpu.make_async_remote_copy(
+        src_ref=src,
+        dst_ref=dst,
+        send_sem=send,
+        recv_sem=recv,
+        device_id=(row, col),
+        device_id_type=MESH,
+    )
+
+
+def fused_kernel(
+    dims,
+    lat_ref,
+    scale_ref,
+    shift_ref,
+    time_ref,
+    bias_ref,
+    one_ref,
+    two_ref,
+    qkv_ref,
+    out_w_ref,
+    stale_ref,
+    next_ref,
+    fresh_ref,
+    w_one,
+    w_two,
+    w_in,
+    w_back,
+    patches,
+    edge_out,
+    edges,
+    strip,
+    acts,
+    raw,
+    res,
+    pairs,
+    att_out,
+    att,
+    stats,
+    groups_of,
+    w_sem,
+    stat_send,
+    stat_recv,
+    row_send,
+    row_recv,
+    edge_send,
+    edge_recv,
+    pair_send,
+    pair_recv,
+):
+    parties, strips, rows, cols, width, block = dims
+    total = parties * strips
+    rows_all = parties * rows
+    cells = rows * cols
+    strip_cells = rows_all * cols
+    halo_cells = rows_all * (cols + 2)
+    size = width // GROUPS
+    count = float(strip_cells * strips * size)
+    row_me, col_me = lax.axis_index("prow"), lax.axis_index("pcol")
+    me = row_me * strips + col_me
+    pad = edge_out.shape[1]
+    parts = width // LANES
+
+    def peer(k):
+        other = lax.rem(me + k, total)
+        return lax.div(other, strips), lax.rem(other, strips)
+
+    barrier = pltpu.get_barrier_semaphore()
+    for k in range(1, total):
+        pl.semaphore_signal(barrier, inc=1, device_id=peer(k), device_id_type=MESH)
+
+    taps = [(a, b) for a in range(3) for b in range(3)]
+    loads = [
+        [
+            pltpu.make_async_copy(ref.at[a, b], buf.at[3 * a + b], w_sem.at[9 * which + 3 * a + b])
+            for a, b in taps
+        ]
+        for which, (ref, buf) in enumerate(((one_ref, w_one), (two_ref, w_two)))
+    ]
+    for load in loads[0]:
+        load.start()
+    load_in = pltpu.make_async_copy(qkv_ref, w_in, w_sem.at[18])
+    load_back = pltpu.make_async_copy(out_w_ref, w_back.at[row_me], w_sem.at[19])
+    load_back.start()
+    for load in loads[1]:
+        load.start()
+    load_in.start()
+
+    channel = iota2((width, 128), 0)
+    group = iota2((width, 128), 1) * size
+    groups_of[...] = one_hot((channel >= group) & (channel < group + size))
+    channel = iota2((block, 128), 0) + row_me * block
+    group = iota2((block, 128), 1) * size
+    block_groups = one_hot((channel >= group) & (channel < group + size))
+
+    def send_stats(which, field, members):
+        sums = jnp.concatenate(
+            [
+                jnp.sum(field, axis=0, keepdims=True),
+                jnp.sum(field * field, axis=0, keepdims=True),
+                jnp.zeros((6, field.shape[1]), F32),
+            ],
+            axis=0,
+        )
+        gathered = sum(matmul(term, members) for term in split_terms(sums))
+        stats[which, 0] = gathered[:2]
+
+    def stat_copies(which):
+        return [
+            remote(
+                stats.at[which, 0],
+                stats.at[which, k],
+                stat_send.at[which, k],
+                stat_recv.at[which, k],
+                *peer(k),
+            )
+            for k in range(1, total)
+        ]
+
+    def norm(which, field):
+        both = jnp.sum(stats[which], axis=0) / count
+        average = both[0:1]
+        inverse = lax.rsqrt(both[1:2] - average * average + EPSILON)
+        line = jnp.concatenate([average, inverse, jnp.zeros((6, 128), F32)], axis=0)
+        wide = sum(times_rows(term, groups_of[...]) for term in split_terms(line))
+        gain = wide[1:2] * scale_ref[which : which + 1]
+        return (field - wide[0:1]) * gain + shift_ref[which : which + 1]
+
+    def mine(field):
+        picked = field[:, :block]
+        for other in range(1, parties):
+            part = field[:, other * block : (other + 1) * block]
+            picked = jnp.where(row_me == other, part, picked)
+        return picked
+
+    own = jnp.concatenate([lat_ref[i].astype(F32) for i in range(rows)], axis=0)
+    own_b = own.astype(BF)
+    patches[row_me] = own_b
+    send_stats(0, own, groups_of[...])
+    packed = jnp.zeros((2 * pad, LANES), F32)
+    for j in range(parts):
+        at, source = iota2((2 * pad, cells), 0), iota2((2 * pad, cells), 1)
+        side = jnp.where(at >= pad, 1, 0)
+        row = at - side * pad - j * rows
+        wanted = row * cols + side * (cols - 1)
+        chosen = one_hot((source == wanted) & (row >= 0) & (row < rows))
+        packed = packed + matmul(chosen, own_b[:, j * LANES : (j + 1) * LANES])
+    edge_out[0] = packed[:pad].astype(BF)
+    edge_out[1] = packed[pad:].astype(BF)
+
+    @pl.when(col_me == 0)
+    def _():
+        edges[0] = jnp.zeros(edges.shape[1:], BF)
+
+    @pl.when(col_me == strips - 1)
+    def _():
+        edges[1] = jnp.zeros(edges.shape[1:], BF)
+
+    pl.semaphore_wait(barrier, total - 1)
+
+    def along(k):
+        return lax.rem(row_me + k, parties)
+
+    def row_copies(which, pick_src, pick_dst):
+        return [
+            remote(
+                pick_src(along(k)),
+                pick_dst(row_me),
+                row_send.at[which, k],
+                row_recv.at[which, k],
+                along(k),
+                col_me,
+            )
+            for k in range(1, parties)
+        ]
+
+    def edge_copies(which, src, dst):
+        return [
+            [
+                remote(
+                    src(side),
+                    dst(1 - side),
+                    edge_send.at[which, side, k],
+                    edge_recv.at[which, side, k],
+                    along(k),
+                    jnp.maximum(col_me - 1, 0)
+                    if side == 0
+                    else jnp.minimum(col_me + 1, strips - 1),
+                )
+                for k in range(parties)
+            ]
+            for side in range(2)
+        ]
+
+    def run_edges(copies, action):
+        for side in range(2):
+            sends = (col_me > 0) if side == 0 else (col_me < strips - 1)
+            takes = (col_me < strips - 1) if side == 0 else (col_me > 0)
+
+            @pl.when(takes if action == "recv" else sends)
+            def _():
+                for copy in copies[side]:
+                    if action == "start":
+                        copy.start()
+                    elif action == "recv":
+                        copy.wait_recv()
+                    else:
+                        copy.wait_send()
+
+    stat0 = stat_copies(0)
+    patch0 = row_copies(0, lambda t: patches.at[row_me], lambda me_row: patches.at[me_row])
+    edge0 = edge_copies(0, lambda s: edge_out.at[s], lambda s: edges.at[s, row_me])
+    for copy in stat0:
+        copy.start()
+    for copy in patch0:
+        copy.start()
+    run_edges(edge0, "start")
+
+    for copy in patch0:
+        copy.wait_recv()
+    run_edges(edge0, "recv")
+
+    at, source = iota2((strip_cells, strip_cells), 0), iota2((strip_cells, strip_cells), 1)
+    at_col, at_row = lax.div(at, rows_all), lax.rem(at, rows_all)
+    to_columns = one_hot(source == at_row * cols + at_col)
+    at_row, at_col = lax.div(at, cols), lax.rem(at, cols)
+    to_rows = one_hot(source == at_col * rows_all + at_row)
+
+    strip[rows_all : rows_all + strip_cells] = matmul(
+        to_columns, patches[...].reshape(strip_cells, width)
+    )
+    arrived = edges[...].reshape(2 * parties * pad, LANES)
+    at = iota2((2 * rows_all, 2 * parties * pad), 0)
+    source = iota2((2 * rows_all, 2 * parties * pad), 1)
+    for j in range(parts):
+        chosen = one_hot(source == lax.div(at, rows) * pad + j * rows + lax.rem(at, rows))
+        part = matmul(chosen, arrived)
+        span = slice(j * LANES, (j + 1) * LANES)
+        strip[:rows_all, span] = part[:rows_all]
+        strip[rows_all + strip_cells :, span] = part[rows_all:]
+
+    for copy in stat0:
+        copy.wait_recv()
+
+    where_at = iota2((halo_cells, 1), 0)
+    outside = ((where_at < rows_all) & (col_me == 0)) | (
+        (where_at >= rows_all + strip_cells) & (col_me == strips - 1)
+    )
+    in_column = lax.rem(where_at, rows_all)
+
+    def activate(which, field):
+        normed = norm(which, field)
+        act = jnp.where(outside, 0.0, normed / (1.0 + jnp.exp(-normed)))
+        acts[1] = act.astype(BF)
+        acts[0] = jnp.where(in_column == 0, 0.0, pltpu.roll(act, 1, 0)).astype(BF)
+        acts[2] = jnp.where(
+            in_column == rows_all - 1, 0.0, pltpu.roll(act, halo_cells - 1, 0)
+        ).astype(BF)
+
+    def convolve(which, weights):
+        result = jnp.zeros((strip_cells, block), F32)
+        for a, b in taps:
+            loads[which][3 * a + b].wait()
+            result = result + times_rows(
+                acts[a, b * rows_all : b * rows_all + strip_cells], weights[3 * a + b]
+            )
+        return result
+
+    activate(0, strip[...])
+
+    load_back.wait()
+    back = row_copies(3, lambda t: w_back.at[row_me], lambda me_row: w_back.at[me_row])
+    pair_copies = [
+        remote(
+            stale_ref,
+            pairs.at[col_me],
+            pair_send.at[k],
+            pair_recv.at[k],
+            row_me,
+            lax.rem(col_me + k, strips),
+        )
+        for k in range(1, strips)
+    ]
+    for copy in pair_copies:
+        copy.start()
+    for copy in back:
+        copy.start()
+
+    first = convolve(0, w_one)
+    offset = bias_ref[0:1] + time_ref[...]
+    middle = pl.ds(rows_all, strip_cells)
+    raw[row_me, rows_all : rows_all + strip_cells] = first.astype(BF)
+    raw1 = row_copies(1, lambda t: raw.at[row_me, middle], lambda me_row: raw.at[me_row, middle])
+    ends_src = (pl.ds(rows_all, rows_all), pl.ds(strip_cells, rows_all))
+    ends_dst = (pl.ds(0, rows_all), pl.ds(rows_all + strip_cells, rows_all))
+    edge1 = edge_copies(
+        1, lambda s: raw.at[row_me, ends_src[s]], lambda s: raw.at[row_me, ends_dst[s]]
+    )
+    for copy in raw1:
+        copy.start()
+    run_edges(edge1, "start")
+    send_stats(1, first + mine(offset), block_groups)
+    stat1 = stat_copies(1)
+    for copy in stat1:
+        copy.start()
+
+    @pl.when(col_me == 0)
+    def _():
+        raw[:, :rows_all] = jnp.zeros((parties, rows_all, block), BF)
+
+    @pl.when(col_me == strips - 1)
+    def _():
+        raw[:, rows_all + strip_cells :] = jnp.zeros((parties, rows_all, block), BF)
+
+    residual = mine(strip[rows_all : rows_all + strip_cells]) + mine(bias_ref[1:2])
+
+    for copy in raw1:
+        copy.wait_recv()
+    run_edges(edge1, "recv")
+    field = jnp.concatenate([raw[i].astype(F32) for i in range(parties)], axis=1) + offset
+    for copy in stat1:
+        copy.wait_recv()
+    activate(1, field)
+    second = convolve(1, w_two)
+
+    rounded = (residual + second).astype(BF)
+    res[row_me] = rounded
+    res2 = row_copies(2, lambda t: res.at[row_me], lambda me_row: res.at[me_row])
+    for copy in res2:
+        copy.start()
+    send_stats(2, rounded.astype(F32), block_groups)
+    stat2 = stat_copies(2)
+    for copy in stat2:
+        copy.start()
+    for copy in res2:
+        copy.wait_recv()
+    field = jnp.concatenate([res[i].astype(F32) for i in range(parties)], axis=1)
+    at, source = iota2((cells, strip_cells), 0), iota2((cells, strip_cells), 1)
+    patch_row = row_me * rows + lax.div(at, cols)
+    chosen = one_hot(source == lax.rem(at, cols) * rows_all + patch_row)
+    kept = matmul(chosen, field.astype(BF))
+    load_in.wait()
+    for copy in stat2:
+        copy.wait_recv()
+    attn_in = norm(2, field).astype(BF)
+
+    queries = times_rows(attn_in, w_in[:HEAD]).astype(BF)
+    fresh = times_rows(attn_in, w_in[HEAD:]).astype(BF)
+    for copy in pair_copies:
+        copy.wait_recv()
+    pairs[col_me] = fresh
+    fresh_ref[...] = matmul(to_rows, fresh).astype(BF)
+    both = pairs[...].reshape(strips * strip_cells, 2 * HEAD)
+    scores = times_rows(queries, both[:, :HEAD]) * (HEAD**-0.5)
+    weights = jnp.exp(scores - jnp.max(scores, axis=1, keepdims=True))
+    denominator = jnp.sum(weights, axis=1, keepdims=True)
+    attended = (matmul(weights.astype(BF), both) / denominator)[:, HEAD:].astype(BF)
+    att_out[...] = (
+        matmul(to_rows, attended).astype(BF).reshape(parties, cells, HEAD)
+    )
+    att3 = row_copies(4, lambda t: att_out.at[t], lambda me_row: att.at[me_row])
+    for copy in att3:
+        copy.start()
+    att[row_me] = att_out[row_me]
+    for copy in back:
+        copy.wait_recv()
+    for copy in att3:
+        copy.wait_recv()
+    heads = jnp.concatenate([att[i].astype(F32) for i in range(parties)], axis=1).astype(BF)
+    added = jnp.concatenate([times_rows(heads, w_back[i]) for i in range(parties)], axis=1)
+    result = kept + added
+    for i in range(rows):
+        next_ref[i] = result[i * cols : (i + 1) * cols].astype(BF)
+
+    for copy in stat0 + stat1 + stat2 + patch0 + raw1 + res2 + back + att3 + pair_copies:
+        copy.wait_send()
+    run_edges(edge0, "send")
+    run_edges(edge1, "send")
+
+
+def fused(
+    latent,
+    norm_scale,
+    norm_shift,
+    time_shift,
+    conv_bias,
+    conv_one,
+    conv_two,
+    w_qkv,
+    w_out,
+    stale_kv,
+):
+    rows, cols, width = latent.shape
+    block = conv_one.shape[2]
+    parties, strips = lax.axis_size("prow"), lax.axis_size("pcol")
+    total = parties * strips
+    rows_all = rows * parties
+    cells = rows * cols
+    strip_cells = rows_all * cols
+    halo_cells = rows_all * (cols + 2)
+    pad = -(-rows * (width // LANES) // 16) * 16
+    dims = (parties, strips, rows, cols, width, block)
+    vmem = pl.BlockSpec(memory_space=pltpu.VMEM)
+    anywhere = pl.BlockSpec(memory_space=pl.ANY)
+    dma = pltpu.SemaphoreType.DMA
+    next_latent, fresh = pl.pallas_call(
+        functools.partial(fused_kernel, dims),
+        out_shape=(
+            jax.ShapeDtypeStruct(latent.shape, BF),
+            jax.ShapeDtypeStruct((strip_cells, 2 * HEAD), BF),
+        ),
+        in_specs=[vmem] * 5 + [anywhere] * 4 + [vmem],
+        out_specs=(vmem, vmem),
+        scratch_shapes=[
+            pltpu.VMEM((9, block, width), BF),
+            pltpu.VMEM((9, block, width), BF),
+            pltpu.VMEM(w_qkv.shape, BF),
+            pltpu.VMEM((parties,) + w_out.shape, BF),
+            pltpu.VMEM((parties, cells, width), BF),
+            pltpu.VMEM((2, pad, LANES), BF),
+            pltpu.VMEM((2, parties, pad, LANES), BF),
+            pltpu.VMEM((halo_cells, width), F32),
+            pltpu.VMEM((3, halo_cells, width), BF),
+            pltpu.VMEM((parties, halo_cells, block), BF),
+            pltpu.VMEM((parties, strip_cells, block), BF),
+            pltpu.VMEM((strips, strip_cells, 2 * HEAD), BF),
+            pltpu.VMEM((parties, cells, HEAD), BF),
+            pltpu.VMEM((parties, cells, HEAD), BF),
+            pltpu.VMEM((3, total, 2, 128), F32),
+            pltpu.VMEM((width, 128), BF),
+            dma((20,)),
+            dma((3, total)),
+            dma((3, total)),
+            dma((5, parties)),
+            dma((5, parties)),
+            dma((2, 2, parties)),
+            dma((2, 2, parties)),
+            dma((strips,)),
+            dma((strips,)),
+        ],
+        compiler_params=pltpu.CompilerParams(
+            collective_id=0, has_side_effects=True, vmem_limit_bytes=48 * 2**20
+        ),
+    )(
+        latent,
+        norm_scale,
+        norm_shift,
+        time_shift.reshape(1, width),
+        conv_bias,
+        conv_one,
+        conv_two,
+        w_qkv,
+        w_out,
+        stale_kv.reshape(strip_cells, 2 * HEAD),
+    )
+    return next_latent, fresh.reshape(rows_all, cols, 1, 2 * HEAD)
+
+
 def solution(mesh):
     placed = (
         P("prow", "pcol", None),
@@ -187,8 +693,12 @@
         P("prow", None),
         P(None, "pcol", "prow", None),
     )
+
+    def body(*args):
+        return (fused if fits(mesh, *args) else shards)(*args)
+
     return jax.shard_map(
-        shards,
+        body,
         mesh=mesh,
         in_specs=placed,
         out_specs=(P("prow", "pcol", None), P(None, "pcol", "prow", None)),

time: 269 us -> 52.5 us (0.20)
  blocking collectives: 177 us -> 0 us
  Pallas kernels: 0 us -> 43.8 us
  matrix products: 30.5 us -> 0 us
  starting transfers between devices: 25.9 us -> 0 us
  waiting for transfers between devices: 22.6 us -> 0 us
  other arithmetic: 4.62 us -> 0 us
    psum x3 -> x0, blocking collectives: 123 us -> none  [group_norm(): lax.psum((jnp.sum(grouped, axis=(0, 2)), jnp.sum(grouped * grouped, axis=...]
    all_gather x5 -> x0, blocking collectives: 53.8 us -> none  [the longest x2 21.6 us: conv_terms(): stacked = lax.all_gather(framed_patch[None], 'prow', axis=0, tiled=True)]
    pallas_call x0 -> x1, Pallas kernels: none -> 43.8 us  [fused(): pl.pallas_call(functools.partial(fused_kernel, dims), out_shape=(jax.Shap...]
    dot_general x24 -> x0, matrix products: 30.5 us -> none  [the longest x20 29.5 us: times_rows(): lax.dot_general(left, right, (((1,), (1,)), ((), ())), preferred_element_...]
    ppermute x8 -> x0, starting transfers between devices: 16.1 us -> none  [the longest x4 10.9 us: padded(): lax.ppermute(tail, axis, [(i, (i + 1) % count) for i in range(ends)])]
    ppermute x8 -> x0, waiting for transfers between devices: 14 us -> none  [the longest x4 13.8 us: padded(): lax.ppermute(head, axis, [((i + 1) % count, i) for i in range(ends)])]
    all_to_all x3 -> x0, starting transfers between devices: 9.82 us -> none  [the longest x2 6.55 us: conv_terms(): lax.all_to_all(total.reshape(parties, cells, out_width).astype(jnp.bfloat...]
    all_to_all x3 -> x0, waiting for transfers between devices: 8.64 us -> none  [the longest x2 4.56 us: conv_terms(): lax.all_to_all(total.reshape(parties, cells, out_width).astype(jnp.bfloat...]
  transfers between devices with their start and end apart: 11 -> 0, of which waited for: 8 -> 0; matrix products, arithmetic and copies ran while one was open for 0% -> 0% of each run, Pallas kernels for 0% -> 0%
where the time goes in v1:
time: 52.5 us; the launch traced here: 52 us
  Pallas kernels  43.8 us (83%)
  local copies, waits for them, and re-layouts  7.52 us (14%)
  between operations  0.65 us (1%)
    pallas_call x1, Pallas kernels, fused(): pl.pallas_call(functools.partial(fused_kernel, dims), out_shape=(jax.Shap...  43.8 us
    unnamed x16, local copies, waits for them, and re-layouts  6.82 us

profile of v1, /device:TPU:0, one launch (start us, length us, event | category | flops | bytes accessed | tf_op | source)
XLA Modules:
  0.0 52.0 jit_solution(10670587905400344434)
XLA Ops:
  0.6 0.7 %reshape.13.time_ref = f32[1,1280]{1,0:T(1,128)S(1)} reshape(f32[1280]{0:T(1024)} %param.13) | data formatting | bytes 10240 | tf_op jit(solution)/shard_map/reshape | solution.py:672
  1.3 0.0 copy-start
  1.3 1.0 %copy-done = bf16[192,1280]{1,0:T(8,128)(2,1)S(1)} copy-done((bf16[192,1280]{1,0:T(8,128)(2,1)S(1)}, bf16[192,1280]{1,0:T(8,128)(2,1)}, u32[]{:S(2)}) %copy-start) | copy-done | bytes 491544
  2.4 0.0 copy-start.1
  2.4 0.9 %copy-done.1 = bf16[320,256]{1,0:T(8,128)(2,1)S(1)} copy-done((bf16[320,256]{1,0:T(8,128)(2,1)S(1)}, bf16[320,256]{1,0:T(8,128)(2,1)}, u32[]{:S(2)}) %copy-start.1) | copy-done | bytes 163864
  3.3 0.0 copy-start.2
  3.3 0.8 %copy-done.2 = bf16[4,4,1280]{2,1,0:T(4,128)(2,1)S(1)} copy-done((bf16[4,4,1280]{2,1,0:T(4,128)(2,1)S(1)}, bf16[4,4,1280]{2,1,0:T(4,128)(2,1)}, u32[]{:S(2)}) %copy-start.2) | copy-done | bytes 40984
  4.1 0.0 copy-start.3
  4.1 0.7 %copy-done.3 = f32[3,1280]{1,0:T(4,128)S(1)} copy-done((f32[3,1280]{1,0:T(4,128)S(1)}, f32[3,1280]{1,0:T(4,128)}, u32[]{:S(2)}) %copy-start.3) | copy-done | bytes 15384
  4.8 0.0 copy-start.4
  4.8 0.7 %copy-done.4 = f32[3,1280]{1,0:T(4,128)S(1)} copy-done((f32[3,1280]{1,0:T(4,128)S(1)}, f32[3,1280]{1,0:T(4,128)}, u32[]{:S(2)}) %copy-start.4) | copy-done | bytes 15384
  5.5 0.0 copy-start.5
  5.5 0.7 %copy-done.5 = bf16[16,4,1,128]{3,1,2,0:T(4,128)(2,1)S(1)} copy-done((bf16[16,4,1,128]{3,1,2,0:T(4,128)(2,1)S(1)}, bf16[16,4,1,128]{3,1,2,0:T(4,128)(2,1)}, u32[]{:S(2)}) %copy-start.5) | copy-done | bytes 16408
  6.2 0.0 copy-start.6
  6.2 0.7 %copy-done.6 = f32[2,1280]{1,0:T(2,128)S(1)} copy-done((f32[2,1280]{1,0:T(2,128)S(1)}, f32[2,1280]{1,0:T(2,128)}, u32[]{:S(2)}) %copy-start.6) | copy-done | bytes 10264
  6.9 43.8 %shard_map.113 = (bf16[4,4,1280]{2,1,0:T(4,128)(2,1)S(1)}, bf16[64,128]{1,0:T(8,128)(2,1)S(1)}) custom-call(bf16[4,4,1280]{2,1,0:T(4,128)(2,1)S(1)} %copy-done.2, f32[3,1280]{1,0:T(4,128)S(1)} %copy-done.3, f32[3,1280]{1,0:T(4,128)S(1)} %copy-done.4, f32[1,1280]{1,0:T(1,128)S(1)} %reshape.13.time_ref, f32[2,1280]{1,0:T(2,128)S(1)} %copy-done.6, ...), custom_call_target="tpu_custom_call" | custom-call | tf_op jit(solution)/shard_map/pallas_call | solution.py:630
  50.8 0.6 %copy.15 = bf16[4,4,1280]{2,1,0:T(4,128)(2,1)} copy(bf16[4,4,1280]{2,1,0:T(4,128)(2,1)S(1)} %get-tuple-element.10) | data formatting | bytes 81920
  51.4 0.6 %copy.16 = bf16[16,4,1,128]{3,1,2,0:T(4,128)(2,1)} copy(bf16[16,4,1,128]{3,1,2,0:T(4,128)(2,1)S(1)} %bitcast.4) | data formatting | bytes 32768
Async XLA Ops:
  1.3 1.0 %copy-start = (bf16[192,1280]{1,0:T(8,128)(2,1)S(1)}, bf16[192,1280]{1,0:T(8,128)(2,1)}, u32[]{:S(2)}) copy-start(bf16[192,1280]{1,0:T(8,128)(2,1)} %qkv_ref.1) | copy-start | bytes 1474564
  2.4 0.9 %copy-start.1 = (bf16[320,256]{1,0:T(8,128)(2,1)S(1)}, bf16[320,256]{1,0:T(8,128)(2,1)}, u32[]{:S(2)}) copy-start(bf16[320,256]{1,0:T(8,128)(2,1)} %out_w_ref.1) | copy-start | bytes 491524
  3.3 0.8 %copy-start.2 = (bf16[4,4,1280]{2,1,0:T(4,128)(2,1)S(1)}, bf16[4,4,1280]{2,1,0:T(4,128)(2,1)}, u32[]{:S(2)}) copy-start(bf16[4,4,1280]{2,1,0:T(4,128)(2,1)} %lat_ref.1) | copy-start | bytes 122884
  4.1 0.7 %copy-start.3 = (f32[3,1280]{1,0:T(4,128)S(1)}, f32[3,1280]{1,0:T(4,128)}, u32[]{:S(2)}) copy-start(f32[3,1280]{1,0:T(4,128)} %scale_ref.1) | copy-start | bytes 46084
  4.8 0.7 %copy-start.4 = (f32[3,1280]{1,0:T(4,128)S(1)}, f32[3,1280]{1,0:T(4,128)}, u32[]{:S(2)}) copy-start(f32[3,1280]{1,0:T(4,128)} %shift_ref.1) | copy-start | bytes 46084
  5.5 0.7 %copy-start.5 = (bf16[16,4,1,128]{3,1,2,0:T(4,128)(2,1)S(1)}, bf16[16,4,1,128]{3,1,2,0:T(4,128)(2,1)}, u32[]{:S(2)}) copy-start(bf16[16,4,1,128]{3,1,2,0:T(4,128)(2,1)} %param.19) | copy-start | bytes 49156
  6.2 0.7 %copy-start.6 = (f32[2,1280]{1,0:T(2,128)S(1)}, f32[2,1280]{1,0:T(2,128)}, u32[]{:S(2)}) copy-start(f32[2,1280]{1,0:T(2,128)} %bias_ref.1) | copy-start | bytes 30724

commit v2 on v1

--- a/solution.py
+++ b/solution.py
@@ -195,6 +195,7 @@
         and (rows * cols) % 16 == 0
         and width % LANES == 0
         and block % (width // GROUPS) == 0
+        and block % 32 == 0
         and w_qkv.shape[0] == 3 * HEAD
         and w_out.shape[0] == block
         and 4 * conv_one.size < 32 * 2**20
@@ -234,11 +235,11 @@
 
 def fused_kernel(
     dims,
-    lat_ref,
-    scale_ref,
-    shift_ref,
-    time_ref,
-    bias_ref,
+    lat_in,
+    scale_in,
+    shift_in,
+    time_in,
+    bias_in,
     one_ref,
     two_ref,
     qkv_ref,
@@ -246,6 +247,11 @@
     stale_ref,
     next_ref,
     fresh_ref,
+    lat_ref,
+    scale_ref,
+    shift_ref,
+    time_ref,
+    bias_ref,
     w_one,
     w_two,
     w_in,
@@ -289,6 +295,20 @@
         other = lax.rem(me + k, total)
         return lax.div(other, strips), lax.rem(other, strips)
 
+    small = [
+        pltpu.make_async_copy(src, dst, w_sem.at[20 + i])
+        for i, (src, dst) in enumerate(
+            (
+                (lat_in, lat_ref),
+                (scale_in, scale_ref),
+                (shift_in, shift_ref),
+                (time_in, time_ref),
+                (bias_in, bias_ref),
+            )
+        )
+    ]
+    for load in small:
+        load.start()
     barrier = pltpu.get_barrier_semaphore()
     for k in range(1, total):
         pl.semaphore_signal(barrier, inc=1, device_id=peer(k), device_id_type=MESH)
@@ -357,6 +377,8 @@
             picked = jnp.where(row_me == other, part, picked)
         return picked
 
+    for load in small:
+        load.wait()
     own = jnp.concatenate([lat_ref[i].astype(F32) for i in range(rows)], axis=0)
     own_b = own.astype(BF)
     patches[row_me] = own_b
@@ -440,60 +462,6 @@
         copy.start()
     run_edges(edge0, "start")
 
-    for copy in patch0:
-        copy.wait_recv()
-    run_edges(edge0, "recv")
-
-    at, source = iota2((strip_cells, strip_cells), 0), iota2((strip_cells, strip_cells), 1)
-    at_col, at_row = lax.div(at, rows_all), lax.rem(at, rows_all)
-    to_columns = one_hot(source == at_row * cols + at_col)
-    at_row, at_col = lax.div(at, cols), lax.rem(at, cols)
-    to_rows = one_hot(source == at_col * rows_all + at_row)
-
-    strip[rows_all : rows_all + strip_cells] = matmul(
-        to_columns, patches[...].reshape(strip_cells, width)
-    )
-    arrived = edges[...].reshape(2 * parties * pad, LANES)
-    at = iota2((2 * rows_all, 2 * parties * pad), 0)
-    source = iota2((2 * rows_all, 2 * parties * pad), 1)
-    for j in range(parts):
-        chosen = one_hot(source == lax.div(at, rows) * pad + j * rows + lax.rem(at, rows))
-        part = matmul(chosen, arrived)
-        span = slice(j * LANES, (j + 1) * LANES)
-        strip[:rows_all, span] = part[:rows_all]
-        strip[rows_all + strip_cells :, span] = part[rows_all:]
-
-    for copy in stat0:
-        copy.wait_recv()
-
-    where_at = iota2((halo_cells, 1), 0)
-    outside = ((where_at < rows_all) & (col_me == 0)) | (
-        (where_at >= rows_all + strip_cells) & (col_me == strips - 1)
-    )
-    in_column = lax.rem(where_at, rows_all)
-
-    def activate(which, field):
-        normed = norm(which, field)
-        act = jnp.where(outside, 0.0, normed / (1.0 + jnp.exp(-normed)))
-        acts[1] = act.astype(BF)
-        acts[0] = jnp.where(in_column == 0, 0.0, pltpu.roll(act, 1, 0)).astype(BF)
-        acts[2] = jnp.where(
-            in_column == rows_all - 1, 0.0, pltpu.roll(act, halo_cells - 1, 0)
-        ).astype(BF)
-
-    def convolve(which, weights):
-        result = jnp.zeros((strip_cells, block), F32)
-        for a, b in taps:
-            loads[which][3 * a + b].wait()
-            result = result + times_rows(
-                acts[a, b * rows_all : b * rows_all + strip_cells], weights[3 * a + b]
-            )
-        return result
-
-    activate(0, strip[...])
-
-    load_back.wait()
-    back = row_copies(3, lambda t: w_back.at[row_me], lambda me_row: w_back.at[me_row])
     pair_copies = [
         remote(
             stale_ref,
@@ -505,13 +473,77 @@
         )
         for k in range(1, strips)
     ]
+    half = block // 2
+    halves = (pl.ds(0, half), pl.ds(half, half))
+    back = [
+        row_copies(
+            3 + part,
+            lambda t: w_back.at[row_me, halves[part]],
+            lambda me_row: w_back.at[me_row, halves[part]],
+        )
+        for part in range(2)
+    ]
+
+    for copy in patch0:
+        copy.wait_recv()
+    run_edges(edge0, "recv")
+
+    load_back.wait()
     for copy in pair_copies:
         copy.start()
-    for copy in back:
-        copy.start()
+    for copy in back[0]:
+        copy.start()
+
+    at, source = iota2((strip_cells, strip_cells), 0), iota2((strip_cells, strip_cells), 1)
+    at_col, at_row = lax.div(at, rows_all), lax.rem(at, rows_all)
+    to_columns = one_hot(source == at_row * cols + at_col)
+    at_row, at_col = lax.div(at, cols), lax.rem(at, cols)
+    to_rows = one_hot(source == at_col * rows_all + at_row)
+
+    strip[rows_all : rows_all + strip_cells] = matmul(
+        to_columns, patches[...].reshape(strip_cells, width)
+    )
+    arrived = edges[...].reshape(2 * parties * pad, LANES)
+    at = iota2((2 * rows_all, 2 * parties * pad), 0)
+    source = iota2((2 * rows_all, 2 * parties * pad), 1)
+    for j in range(parts):
+        chosen = one_hot(source == lax.div(at, rows) * pad + j * rows + lax.rem(at, rows))
+        part = matmul(chosen, arrived)
+        span = slice(j * LANES, (j + 1) * LANES)
+        strip[:rows_all, span] = part[:rows_all]
+        strip[rows_all + strip_cells :, span] = part[rows_all:]
+
+    for copy in stat0:
+        copy.wait_recv()
+
+    where_at = iota2((halo_cells, 1), 0)
+    outside = ((where_at < rows_all) & (col_me == 0)) | (
+        (where_at >= rows_all + strip_cells) & (col_me == strips - 1)
+    )
+    in_column = lax.rem(where_at, rows_all)
+
+    def activate(which, field):
+        normed = norm(which, field)
+        act = jnp.where(outside, 0.0, normed / (1.0 + jnp.exp(-normed)))
+        acts[1] = act.astype(BF)
+        acts[0] = jnp.where(in_column == 0, 0.0, pltpu.roll(act, 1, 0)).astype(BF)
+        acts[2] = jnp.where(
+            in_column == rows_all - 1, 0.0, pltpu.roll(act, halo_cells - 1, 0)
+        ).astype(BF)
+
+    def convolve(which, weights):
+        result = jnp.zeros((strip_cells, block), F32)
+        for a, b in taps:
+            loads[which][3 * a + b].wait()
+            result = result + times_rows(
+                acts[a, b * rows_all : b * rows_all + strip_cells], weights[3 * a + b]
+            )
+        return result
+
+    activate(0, strip[...])
 
     first = convolve(0, w_one)
-    offset = bias_ref[0:1] + time_ref[...]
+    offset = bias_ref[0:1] + time_ref[...].reshape(1, width)
     middle = pl.ds(rows_all, strip_cells)
     raw[row_me, rows_all : rows_all + strip_cells] = first.astype(BF)
     raw1 = row_copies(1, lambda t: raw.at[row_me, middle], lambda me_row: raw.at[me_row, middle])
@@ -541,6 +573,8 @@
     for copy in raw1:
         copy.wait_recv()
     run_edges(edge1, "recv")
+    for copy in back[1]:
+        copy.start()
     field = jnp.concatenate([raw[i].astype(F32) for i in range(parties)], axis=1) + offset
     for copy in stat1:
         copy.wait_recv()
@@ -582,11 +616,11 @@
     att_out[...] = (
         matmul(to_rows, attended).astype(BF).reshape(parties, cells, HEAD)
     )
-    att3 = row_copies(4, lambda t: att_out.at[t], lambda me_row: att.at[me_row])
+    att3 = row_copies(5, lambda t: att_out.at[t], lambda me_row: att.at[me_row])
     for copy in att3:
         copy.start()
     att[row_me] = att_out[row_me]
-    for copy in back:
+    for copy in back[0] + back[1]:
         copy.wait_recv()
     for copy in att3:
         copy.wait_recv()
@@ -596,7 +630,7 @@
     for i in range(rows):
         next_ref[i] = result[i * cols : (i + 1) * cols].astype(BF)
 
-    for copy in stat0 + stat1 + stat2 + patch0 + raw1 + res2 + back + att3 + pair_copies:
+    for copy in stat0 + stat1 + stat2 + patch0 + raw1 + res2 + back[0] + back[1] + att3 + pair_copies:
         copy.wait_send()
     run_edges(edge0, "send")
     run_edges(edge1, "send")
@@ -625,7 +659,7 @@
     pad = -(-rows * (width // LANES) // 16) * 16
     dims = (parties, strips, rows, cols, width, block)
     vmem = pl.BlockSpec(memory_space=pltpu.VMEM)
-    anywhere = pl.BlockSpec(memory_space=pl.ANY)
+    hbm = pl.BlockSpec(memory_space=pltpu.HBM)
     dma = pltpu.SemaphoreType.DMA
     next_latent, fresh = pl.pallas_call(
         functools.partial(fused_kernel, dims),
@@ -633,9 +667,14 @@
             jax.ShapeDtypeStruct(latent.shape, BF),
             jax.ShapeDtypeStruct((strip_cells, 2 * HEAD), BF),
         ),
-        in_specs=[vmem] * 5 + [anywhere] * 4 + [vmem],
+        in_specs=[hbm] * 10,
         out_specs=(vmem, vmem),
         scratch_shapes=[
+            pltpu.VMEM(latent.shape, BF),
+            pltpu.VMEM(norm_scale.shape, F32),
+            pltpu.VMEM(norm_shift.shape, F32),
+            pltpu.VMEM(time_shift.shape, F32),
+            pltpu.VMEM(conv_bias.shape, F32),
             pltpu.VMEM((9, block, width), BF),
             pltpu.VMEM((9, block, width), BF),
             pltpu.VMEM(w_qkv.shape, BF),
@@ -652,24 +691,24 @@
             pltpu.VMEM((parties, cells, HEAD), BF),
             pltpu.VMEM((3, total, 2, 128), F32),
             pltpu.VMEM((width, 128), BF),
-            dma((20,)),
+            dma((25,)),
             dma((3, total)),
             dma((3, total)),
-            dma((5, parties)),
-            dma((5, parties)),
+            dma((6, parties)),
+            dma((6, parties)),
             dma((2, 2, parties)),
             dma((2, 2, parties)),
             dma((strips,)),
             dma((strips,)),
         ],
         compiler_params=pltpu.CompilerParams(
-            collective_id=0, has_side_effects=True, vmem_limit_bytes=48 * 2**20
+            collective_id=0, has_side_effects=True, vmem_limit_bytes=63 * 2**20
         ),
     )(
         latent,
         norm_scale,
         norm_shift,
-        time_shift.reshape(1, width),
+        time_shift,
         conv_bias,
         conv_one,
         conv_two,

time: 52.5 us -> 44.6 us (0.85)
  local copies, waits for them, and re-layouts: 7.52 us -> 2.74 us
  Pallas kernels: 43.8 us -> 41 us
    unnamed x16 -> x2, local copies, waits for them, and re-layouts: 6.82 us -> 2.74 us
    pallas_call x1, Pallas kernels: 43.8 us -> 41 us  [fused(): pl.pallas_call(functools.partial(fused_kernel, dims), out_shape=(jax.Shap...]
    reshape x1 -> x0, local copies, waits for them, and re-layouts: 0.7 us -> none  [fused(): time_shift.reshape(1, width)]
where the time goes in v2:
time: 44.6 us; the launch traced here: 44.4 us
  Pallas kernels  41 us (92%)
  local copies, waits for them, and re-layouts  2.74 us (6%)
  between operations  0.64 us (1%)
    pallas_call x1, Pallas kernels, fused(): pl.pallas_call(functools.partial(fused_kernel, dims), out_shape=(jax.Shap...  41 us
    unnamed x2, local copies, waits for them, and re-layouts  2.74 us

profile of v2, /device:TPU:0, one launch (start us, length us, event | category | flops | bytes accessed | tf_op | source)
XLA Modules:
  0.0 44.4 jit_solution(12842871100621502566)
XLA Ops:
  0.6 41.0 %shard_map.113 = (bf16[4,4,1280]{2,1,0:T(4,128)(2,1)}, bf16[64,128]{1,0:T(8,128)(2,1)}) custom-call(bf16[4,4,1280]{2,1,0:T(4,128)(2,1)} %lat_in.1, f32[3,1280]{1,0:T(4,128)} %scale_in.1, f32[3,1280]{1,0:T(4,128)} %shift_in.1, f32[1280]{0:T(1024)} %time_in.1, f32[2,1280]{1,0:T(2,128)} %bias_in.1, bf16[3,3,320,1280]{3,2,1,0:T(8,128)(2,1)} %one_ref.1, ...), custom_call_target="tpu_custom_call" | custom-call | tf_op jit(solution)/shard_map/pallas_call | solution.py:664
  41.6 1.4 %copy.15 = bf16[4,4,1280]{2,1,0:T(4,128)(2,1)} copy(bf16[4,4,1280]{2,1,0:T(4,128)(2,1)} %get-tuple-element.10) | data formatting | bytes 81920
  43.0 1.3 %copy.16 = bf16[16,4,1,128]{3,1,2,0:T(4,128)(2,1)} copy(bf16[16,4,1,128]{3,1,2,0:T(4,128)(2,1)} %bitcast.5) | data formatting | bytes 32768
